TPU v7x, 128 devices: a whole 4x4x4 slice. The times are simulated.
128 devices in a mesh: section: 64 (over z, y, x), tp: 2 (over core).
Axes of the slice: x: 4, y: 4, z: 4, core: 2. Of those that a mesh axis runs over, the one named last changes fastest.
Arguments:
- partials: bfloat16 [64, 2, 512, 8192], P('section', 'tp'), may hold values from -30 to 30
- kept_positions: int32 [64, 512], replicated, may hold values from 0 to 4095, as said below
- destination: int32 [64, 512], replicated, may hold values from 0 to 63, as said below
- slot_index: int32 [64, 512], replicated, may hold values from 0 to 511, as said below
- query_scale: float32 [8192], P('tp'), may hold values from -1.5 to 1.5
- key_scale: float32 [8192], P('tp'), may hold values from -1.5 to 1.5
Outputs:
- attended: bfloat16 [32768, 8192], P('section', 'tp')
Inputs may be any that keep to these rules, and one draw needn't show every extreme that they name: `destination`: each source segment sends exactly 8 of its rows to every segment, itself included; every segment receives exactly 512 rows. `slot_index`: the rows arriving at one segment have distinct slots. `kept_positions`: distinct within a segment's microbatch.
All inputs are finite; a program needn't handle non-finite values.
Results may differ from a plain program's by a relative error of at most 0.0075.
Values may be sent and summed in bfloat16 or wider, within the bound.
A program may use at most 192 MiB of HBM per device.

v0:
```python
import math

import jax
import jax.numpy as jnp
from jax import lax
from jax.sharding import PartitionSpec as P

HD = 128
CAP = 8
D = 8192


eps = 1e-05
theta = 500000.0


def rotate(values, positions):
    half = values.shape[-1] // 2
    freq = jnp.exp(
        jnp.arange(half, dtype=jnp.float32) * (-2.0 * math.log(theta) / values.shape[-1])
    )
    angle = positions.astype(jnp.float32)[:, None] * freq[None, :]
    cosine = jnp.cos(angle)[:, None, :]
    sine = jnp.sin(angle)[:, None, :]
    first = values[..., :half]
    second = values[..., half:]
    return jnp.concatenate([first * cosine - second * sine, second * cosine + first * sine], -1)


def attend(rows, sumsq, positions, sources, query_scale, key_scale):
    count = rows.shape[0]
    heads = query_scale.shape[0] // HD
    normed = rows.astype(jnp.float32) * lax.rsqrt(sumsq / D + eps)[:, None]
    query = rotate((normed * query_scale[None, :]).reshape(count, heads, HD), positions).astype(
        jnp.bfloat16
    )
    keys = rotate((normed * key_scale[None, :]).reshape(count, heads, HD), positions).astype(
        jnp.bfloat16
    )
    value = normed.reshape(count, heads, HD).astype(jnp.bfloat16)
    allowed = (sources[None, :] == sources[:, None]) & (positions[None, :] <= positions[:, None])
    scores = jnp.einsum(
        "qhd,khd->hqk", query, keys, preferred_element_type=jnp.float32
    ) / math.sqrt(HD)
    scores = jnp.where(allowed[None], scores, -1e30)
    top = jnp.max(scores, -1, keepdims=True)
    expd = jnp.exp(scores - top)
    weights = (expd / jnp.sum(expd, -1, keepdims=True)).astype(jnp.bfloat16)
    out = jnp.einsum("hqk,khd->qhd", weights, value, preferred_element_type=jnp.float32)
    return out.reshape(count, heads * HD).astype(jnp.bfloat16)


def local(partials, kept_positions, destination, slot_index, query_scale, key_scale):
    kept = partials.shape[2]
    width = partials.shape[3]
    terms = partials.reshape(kept, width)
    total = lax.psum(terms, "tp").astype(jnp.float32)
    share_width = width // lax.axis_size("tp")
    share = lax.dynamic_slice_in_dim(total, lax.axis_index("tp") * share_width, share_width, 1)
    hidden = share.astype(jnp.bfloat16)
    segments = lax.axis_size("section")
    here = lax.axis_index("section")
    outgoing = lax.dynamic_index_in_dim(destination, here, 0, keepdims=False)
    buckets = jnp.arange(segments, dtype=jnp.int32)
    member = (outgoing[:, None] == buckets[None, :]).astype(jnp.int32)
    before = jnp.sum((jnp.cumsum(member, 0) - member) * member, 1)
    target = outgoing * CAP + before
    places = jnp.arange(segments * CAP, dtype=jnp.int32)
    match = (target[None, :] == places[:, None]).astype(jnp.int32)
    source_row = jnp.sum(match * jnp.arange(kept, dtype=jnp.int32)[None, :], 1)
    outbox = jnp.take(hidden, source_row, axis=0)
    inbox = lax.all_to_all(outbox, "section", split_axis=0, concat_axis=0, tiled=True)
    arriving = (destination == here).astype(jnp.int32)
    order = jnp.cumsum(arriving, 1) - arriving
    flat_row = jnp.arange(segments, dtype=jnp.int32)[:, None] * CAP + order
    slots = jnp.arange(kept, dtype=jnp.int32)
    pick = arriving[:, :, None] * (slot_index[:, :, None] == slots[None, None, :]).astype(jnp.int32)
    inbox_row = jnp.sum(pick * flat_row[:, :, None], (0, 1))
    packed_pos = jnp.sum(pick * kept_positions[:, :, None], (0, 1))
    packed_src = inbox_row // CAP
    packed = jnp.take(inbox, inbox_row, axis=0)
    sumsq = lax.psum(jnp.sum(jnp.square(packed.astype(jnp.float32)), 1), "tp")
    return attend(packed, sumsq, packed_pos, packed_src, query_scale, key_scale)


def solution(mesh):
    in_specs = (P("section", "tp", None, None), P(), P(), P(), P("tp"), P("tp"))
    out_specs = P("section", "tp")
    return jax.shard_map(local, mesh=mesh, in_specs=in_specs, out_specs=out_specs, check_vma=False)
```

profile of v0, /device:TPU:1, one launch (start us, length us, event | category | flops | bytes accessed | tf_op | source)
XLA Modules:
  0.0 341.9 jit_solution(8595248613768445556)
XLA Ops:
  6.5 0.0 copy-start
  6.5 0.0 all-reduce.2.cloned.1.call-start
  6.5 0.7 all-reduce.2.cloned.1.call-update
  7.3 0.2 copy-done
  7.5 1.2 reduce-window.14
  8.7 0.2 slice_reduce_fusion
  9.0 1.2 reduce-window.16
  10.2 0.2 slice_reduce_fusion.1
  10.4 0.1 fusion.22
  10.6 0.2 select_reduce_fusion
  10.8 0.1 fusion.23
  11.0 47.1 %all-reduce.2.cloned.1.call-done = bf16[512,8192]{1,0:T(8,128)(2,1)} async-done(((bf16[512,8192]{1,0:T(8,128)(2,1)}), bf16[512,8192]{1,0:T(8,128)(2,1)}) %all-reduce.2.cloned.1.call-update) | async-done | bytes 8388624 | tf_op jit(solution)/shard_map/psum | solution.py:57
  58.1 4.7 %convert_convert_fusion = bf16[512,4096]{1,0:T(8,128)(2,1)} fusion(bf16[512,8192]{1,0:T(8,128)(2,1)} %all-reduce.2.cloned.1.call-done, s32[]{:T(128)S(6)} %select_n.30), kind=kLoop, calls=%fused_computation.26 | loop fusion | flops 4194304 | bytes 8388612 | tf_op jit(solution)/shard_map/convert_element_type | solution.py:60
  62.8 11.3 %gather_fusion = bf16[512,4096]{1,0:T(8,128)(2,1)} fusion(bf16[512,4096]{1,0:T(8,128)(2,1)} %convert_convert_fusion, s32[1024]{0:T(1024)S(1)} %pad_clamp_fusion.1), kind=kCustom, calls=%fused_computation.clone | custom fusion | bytes 8390656 | tf_op jit(solution)/shard_map/jit(_take)/gather | solution.py:71
  74.1 0.0 copy-start.1
  74.1 0.0 copy-start.2
  74.1 4.7 %select_bitcast_fusion = bf16[64,8,4096]{2,1,0:T(8,128)(2,1)} fusion(bf16[512,4096]{1,0:T(8,128)(2,1)} %gather_fusion, pred[512]{0:T(512)(128)(4,1)S(1)} %compare_and_fusion.2), kind=kLoop, calls=%fused_computation.34 | loop fusion | flops 2097152 | bytes 8389120 | tf_op jit(solution)/shard_map/all_to_all | solution.py:72
  78.7 10.6 %all-to-all-start = ((bf16[64,8,4096]{2,1,0:T(8,128)(2,1)}), bf16[64,8,4096]{2,1,0:T(8,128)(2,1)}, u32[]{:S(2)}, u32[]{:S(2)}) async-start(bf16[64,8,4096]{2,1,0:T(8,128)(2,1)} %select_bitcast_fusion), calls=%async_computation | async-start | bytes 8388608 | tf_op jit(solution)/shard_map/all_to_all | solution.py:72
  89.3 0.0 copy-done.1
  89.3 0.0 copy-done.2
  89.3 23.2 %fusion.2 = (s32[512]{0:T(512)S(1)}, s32[512]{0:T(512)S(1)}) fusion(s32[64,512]{1,0:T(8,128)S(1)} %copy-done.1, s32[64,512]{1,0:T(8,128)S(1)} %compare_convert_fusion, s32[64,512]{1,0:T(8,128)S(1)} %copy-done.2, s32[64,512]{1,0:T(8,128)S(1)} %fusion.23), kind=kLoop, calls=%fused_computation.6 | loop fusion | flops 100662272 | bytes 528384 | tf_op jit(solution)/shard_map/reduce_sum | solution.py:79
  112.6 0.3 compare_and_fusion
  112.9 1.0 multiply_cosine_fusion
  113.9 28.9 %all-to-all-done = bf16[64,8,4096]{2,1,0:T(8,128)(2,1)} async-done(((bf16[64,8,4096]{2,1,0:T(8,128)(2,1)}), bf16[64,8,4096]{2,1,0:T(8,128)(2,1)}, u32[]{:S(2)}, u32[]{:S(2)}) %all-to-all-start) | async-done | bytes 4194336 | tf_op jit(solution)/shard_map/all_to_all | solution.py:72
  142.7 0.0 copy-start.3
  142.7 0.0 copy-start.4
  142.7 11.3 %gather_fusion.1 = bf16[512,4096]{1,0:T(8,128)(2,1)} fusion(bf16[512,4096]{1,0:T(8,128)(2,1)} %bitcast.7, s32[1024]{0:T(1024)S(1)} %pad_clamp_fusion), kind=kCustom, calls=%fused_computation.1.clone | custom fusion | bytes 8390656 | tf_op jit(solution)/shard_map/jit(_take)/gather | solution.py:81
  154.1 3.4 %fusion.11 = f32[512]{0:T(512)S(1)} fusion(bf16[512,4096]{1,0:T(8,128)(2,1)} %gather_fusion.1, pred[512]{0:T(512)(128)(4,1)S(1)} %compare_and_fusion.1), kind=kLoop, calls=%fused_computation.21 | loop fusion | flops 8388096 | bytes 4196864 | tf_op jit(solution)/shard_map/reduce_sum | solution.py:82
  157.5 4.0 %psum.15 = f32[512]{0:T(512)S(1)} all-reduce(f32[512]{0:T(512)S(1)} %fusion.11), channel_id=1, replica_groups=mesh['section'=64,'tp'=2] {'tp'}, use_global_device_ids=true, to_apply=%region_9.11 | all-reduce | flops 512 | bytes 4096 | tf_op jit(solution)/shard_map/psum | solution.py:82
  161.5 0.0 copy-done.3
  161.5 0.0 copy-done.4
  161.5 9.8 %fusion.8 = (f32[512,4096]{1,0:T(8,128)}, f32[512,4096]{1,0:T(8,128)}, bf16[512,4096]{1,0:T(8,128)(2,1)}) fusion(f32[4096]{0:T(1024)S(1)} %copy-done.3, f32[512]{0:T(512)S(1)} %add_rsqrt_fusion, bf16[512,4096]{1,0:T(8,128)(2,1)} %gather_fusion.1, pred[512]{0:T(512)(128)(4,1)S(1)} %compare_and_fusion.1, f32[4096]{0:T(1024)S(1)} %copy-done.4), kind=kLoop, calls=%fused_computation.18 | loop fusion | flops 12582912 | bytes 25201152 | tf_op jit(solution)/shard_map/mul | solution.py:37
  171.2 9.0 %copy.29 = f32[512,4096]{0,1:T(8,128)} copy(f32[512,4096]{1,0:T(8,128)} %get-tuple-element.16) | data formatting | bytes 16777216 | tf_op jit(solution)/shard_map/mul | solution.py:37
  180.2 8.7 %fusion.30 = (f32[512,32,64]{0,2,1:T(8,128)}, f32[512,32,64]{0,2,1:T(8,128)}) fusion(f32[512,32,128]{0,2,1:T(8,128)} %bitcast.46), kind=kLoop, calls=%fused_computation.78 | loop fusion | bytes 16777216 | tf_op jit(solution)/shard_map/slice | solution.py:26
  188.9 6.9 %copy.40 = f32[512,32,64]{2,0,1:T(8,128)} copy(f32[512,32,64]{0,2,1:T(8,128)} %get-tuple-element.12) | data formatting | bytes 8388608
  195.8 6.5 %copy.36 = bf16[512,4096]{0,1:T(8,128)(2,1)} copy(bf16[512,4096]{1,0:T(8,128)(2,1)} %get-tuple-element.18) | data formatting | bytes 8388608 | tf_op jit(solution)/shard_map/convert_element_type | solution.py:40
  202.3 6.9 %copy.39 = f32[512,32,64]{2,0,1:T(8,128)} copy(f32[512,32,64]{0,2,1:T(8,128)} %get-tuple-element.13) | data formatting | bytes 8388608
  209.2 9.0 %copy.26 = f32[512,4096]{0,1:T(8,128)} copy(f32[512,4096]{1,0:T(8,128)} %get-tuple-element.17) | data formatting | bytes 16777216 | tf_op jit(solution)/shard_map/mul | solution.py:34
  218.2 8.7 %fusion.31 = (f32[512,32,64]{0,2,1:T(8,128)}, f32[512,32,64]{0,2,1:T(8,128)}) fusion(f32[512,32,128]{0,2,1:T(8,128)} %bitcast.47), kind=kLoop, calls=%fused_computation.79 | loop fusion | bytes 16777216 | tf_op jit(solution)/shard_map/slice | solution.py:26
  226.9 6.9 %copy.38 = f32[512,32,64]{2,0,1:T(8,128)} copy(f32[512,32,64]{0,2,1:T(8,128)} %get-tuple-element.14) | data formatting | bytes 8388608
  233.8 6.9 %copy.37 = f32[512,32,64]{2,0,1:T(8,128)} copy(f32[512,32,64]{0,2,1:T(8,128)} %get-tuple-element.15) | data formatting | bytes 8388608
  240.7 19.4 %subtract_convert_fusion = (bf16[512,32,64]{2,0,1:T(8,128)(2,1)}, bf16[512,32,64]{2,0,1:T(8,128)(2,1)}, bf16[512,32,64]{2,0,1:T(8,128)(2,1)}, bf16[512,32,64]{2,0,1:T(8,128)(2,1)}) fusion(f32[512,32,64]{2,0,1:T(8,128)} %copy.40, f32[512,32,64]{2,0,1:T(8,128)} %copy.39, f32[512,64]{1,0:T(8,128)S(1)} %get-tuple-element.22, ...), kind=kLoop, calls=%fused_computation.23 | loop fusion | flops 16777216 | bytes 25427968 | tf_op jit(solution)/shard_map/convert
  260.0 19.0 %fusion.12 = f32[32,512,512]{1,2,0:T(8,128)} fusion(bf16[512,32,64]{2,0,1:T(8,128)(2,1)} %get-tuple-element.19, bf16[512,32,64]{2,0,1:T(8,128)(2,1)} %get-tuple-element.20, bf16[512,32,64]{2,0,1:T(8,128)(2,1)} %get-tuple-element.9, bf16[512,32,64]{2,0,1:T(8,128)(2,1)} %get-tuple-element.8), kind=kOutput, calls=%fused_computation.27 | convolution fusion | flops 2164260864 | bytes 41943040 | tf_op jit(solution)/shard_map/qhd,khd->hqk/dot_general | solution.py:42
  279.1 34.3 %fusion.32 = (f32[32,512]{1,0:T(8,128)S(1)}, f32[32,512,512]{1,2,0:T(8,128)}) fusion(f32[32,512,512]{1,2,0:T(8,128)} %fusion.12, pred[512,512]{0,1:T(8,128)(4,1)S(1)} %compare_and_fusion), kind=kOutput, calls=%fused_computation.80 | output fusion | flops 50332160 | bytes 67436544 | tf_op jit(solution)/shard_map/sub | solution.py:47
  313.4 15.4 %fusion.19 = bf16[32,128,512]{2,1,0:T(8,128)(2,1)} fusion(bf16[512,32,128]{0,2,1:T(8,128)(2,1)} %bitcast.49, f32[32,512,512]{1,2,0:T(8,128)} %get-tuple-element.26, f32[32,512]{1,0:T(8,128)S(1)} %get-tuple-element.25), kind=kOutput, calls=%fused_computation.36 | convolution fusion | flops 2166358016 | bytes 42008576 | tf_op jit(solution)/shard_map/hqk,khd->qhd/dot_general | solution.py:49
  328.8 6.3 %copy.34 = bf16[512,4096]{1,0:T(8,128)(2,1)} copy(bf16[512,4096]{0,1:T(8,128)(2,1)} %bitcast.50) | data formatting | bytes 8388608 | tf_op jit(solution)/shard_map/convert_element_type | solution.py:50
  (19 shorter events, 0.2 us)
Async XLA Ops:
  6.5 0.9 copy-start
  6.5 51.5 %all-reduce.2.cloned.1.call-start = ((), (), s32[]{:S(2)}) async-start(), calls=%async_computation.1 | async-start | bytes 16777216 | tf_op jit(solution)/shard_map/psum | solution.py:57
  74.1 15.3 %copy-start.1 = (s32[64,512]{1,0:T(8,128)S(1)}, s32[64,512]{1,0:T(8,128)}, u32[]{:S(2)}) copy-start(s32[64,512]{1,0:T(8,128)} %param.9) | copy-start | bytes 393220
  74.1 15.3 %copy-start.2 = (s32[64,512]{1,0:T(8,128)S(1)}, s32[64,512]{1,0:T(8,128)}, u32[]{:S(2)}) copy-start(s32[64,512]{1,0:T(8,128)} %param.11) | copy-start | bytes 393220
  78.7 64.0 %all-to-all-start = ((bf16[64,8,4096]{2,1,0:T(8,128)(2,1)}), bf16[64,8,4096]{2,1,0:T(8,128)(2,1)}, u32[]{:S(2)}, u32[]{:S(2)}) async-start(bf16[64,8,4096]{2,1,0:T(8,128)(2,1)} %select_bitcast_fusion), calls=%async_computation | async-start | bytes 8388608 | tf_op jit(solution)/shard_map/all_to_all | solution.py:72
  142.7 18.8 %copy-start.3 = (f32[4096]{0:T(1024)S(1)}, f32[4096]{0:T(1024)}, u32[]{:S(2)}) copy-start(f32[4096]{0:T(1024)} %param.13) | copy-start | bytes 49156
  142.7 18.8 %copy-start.4 = (f32[4096]{0:T(1024)S(1)}, f32[4096]{0:T(1024)}, u32[]{:S(2)}) copy-start(f32[4096]{0:T(1024)} %param.12) | copy-start | bytes 49156
Sparse Core Ops, SparseCore 0:
  9.9 48.1 all-reduce.1
where the time goes:
time: 343 us; the launch traced here: 342 us
  other arithmetic  104 us (30%)
  local copies, waits for them, and re-layouts  99 us (29%)
  waiting for transfers between devices  76.7 us (22%)
  matrix products  34.4 us (10%)
  between operations  13.5 us (4%)
  starting transfers between devices  10.6 us (3%)
  blocking collectives  3.98 us (1%)
    psum x1, waiting for transfers between devices, local(): total = lax.psum(terms, 'tp').astype(jnp.float32)  47.1 us
    sub x1, other arithmetic, attend(): expd = jnp.exp(scores - top)  34.3 us
    all_to_all x1, waiting for transfers between devices, local(): lax.all_to_all(outbox, 'section', split_axis=0, concat_axis=0, tiled=True)  28.9 us
    unnamed x14, local copies, waits for them, and re-layouts  27.7 us
    reduce_sum x1, other arithmetic, local(): packed_pos = jnp.sum(pick * kept_positions[:, :, None], (0, 1))  23.2 us
    another operation x6, other arithmetic  21.8 us
    dot_general x1, matrix products, attend(): jnp.einsum('qhd,khd->hqk', query, keys, preferred_element_type=jnp.float32)  19 us
    slice x2, local copies, waits for them, and re-layouts, rotate(): second = values[..., half:]  17.4 us
  transfers between devices with their start and end apart: 2, of which 2 were waited for; matrix products, arithmetic and copies ran while one was open for 8% of the time, Pallas kernels for 0%

commit v1 on v0

v1 whole, which is shorter than its diff:
```python
import functools
import math

import jax
import jax.numpy as jnp
import numpy as np
from jax import lax
from jax.experimental import pallas as pl
from jax.experimental.pallas import tpu as pltpu
from jax.sharding import PartitionSpec as P

HD = 128
CAP = 8
EPS = 1e-05
THETA = 500000.0
BLOCK = 128
PAIR = 2 * HD
MESH = pl.DeviceIdType.MESH


def link_load(offset):
    load = [0] * 6
    for axis, step in enumerate(offset):
        if step in (1, 2):
            load[2 * axis] += 1
        if step in (2, 3):
            load[2 * axis + 1] += 1
    return load


def offset_order(side):
    rest = [(a, b, c) for a in range(side) for b in range(side) for c in range(side)][1:]
    total = [0] * 6
    order = []
    while rest:
        def cost(offset):
            load = link_load(offset)
            after = [t + l for t, l in zip(total, load)]
            mean = sum(after) / 6
            return max(after) - min(after), sum((a - mean) ** 2 for a in after), -sum(load)

        best = min(rest, key=cost)
        rest.remove(best)
        total = [t + l for t, l in zip(total, link_load(best))]
        order.append(best)
    return order


def kernel(
    side, rows, width, pieces, early,
    part_ref, pos_ref, dest_ref, slot_ref, qscale_ref, kscale_ref, freq_ref,
    out_ref,
    own, recv, outbox, inbox, result, before_ref, gather_ref, scatter_ref, key_ref,
    posb, slotb, cos_ref, sin_ref, bias_ref, acc, half, half_in, total, total_in, inv_ref, att_ref, scale_ref,
    own_sem, xsend_sem, xrecv_sem, send_sem, recv_sem, hsend_sem, hrecv_sem, tsend_sem, trecv_sem, out_sem,
):
    f32, bf16 = jnp.float32, jnp.bfloat16
    segments = side ** 3
    step = width // pieces
    me = lax.axis_index("section")
    tp = lax.axis_index("tp")
    other = 1 - tp
    here = (me // (side * side), (me // side) % side, me % side)
    order = offset_order(side)

    def peer(offset):
        at = [lax.rem(h + o, side) for h, o in zip(here, offset)]
        return (at[0] * side + at[1]) * side + at[2]

    barrier = pltpu.get_barrier_semaphore()

    def own_copy(c):
        columns = pl.ds(pl.multiple_of(tp * width + c * step, HD), step)
        return pltpu.make_async_copy(part_ref.at[:, columns], own.at[c], own_sem.at[c])

    def exchange(c):
        columns = pl.ds(pl.multiple_of(other * width + c * step, HD), step)
        return pltpu.make_async_remote_copy(
            src_ref=part_ref.at[:, columns], dst_ref=recv.at[c],
            send_sem=xsend_sem.at[c], recv_sem=xrecv_sem.at[c],
            device_id=(me, other), device_id_type=MESH,
        )

    pl.semaphore_signal(barrier, inc=1, device_id=(me, other), device_id_type=MESH)
    for offset in order:
        pl.semaphore_signal(barrier, inc=1, device_id=(peer(offset), tp), device_id_type=MESH)
    for c in range(pieces):
        own_copy(c).start()

    before_ref[...] = (
        lax.broadcasted_iota(jnp.int32, (rows, rows), 0) < lax.broadcasted_iota(jnp.int32, (rows, rows), 1)
    ).astype(f32).astype(bf16)
    mine = dest_ref[pl.ds(me, 1), :]
    member = mine == lax.broadcasted_iota(jnp.int32, (segments, rows), 0)
    ahead = jnp.dot(member.astype(f32).astype(bf16), before_ref[...], preferred_element_type=f32)
    rank = jnp.sum(jnp.where(member, ahead, 0.0), axis=0, keepdims=True)
    target = mine * CAP + rank.astype(jnp.int32)
    gather_ref[...] = (
        lax.broadcasted_iota(jnp.int32, (rows, rows), 0) == target
    ).astype(f32).astype(bf16)
    acc[...] = jnp.zeros_like(acc)

    pl.semaphore_wait(barrier, segments)
    for c in range(pieces):
        exchange(c).start()

    def send_piece(c):
        for offset in order:
            there = peer(offset)
            pltpu.make_async_remote_copy(
                src_ref=outbox.at[c, there], dst_ref=inbox.at[c, me],
                send_sem=send_sem, recv_sem=recv_sem.at[c],
                device_id=(there, tp), device_id_type=MESH,
            ).start()

    def reduce_piece(c):
        own_copy(c).wait()
        exchange(c).wait_recv()

        def strip(i, carry):
            columns = pl.ds(pl.multiple_of(i * PAIR, PAIR), PAIR)
            summed = (own[c, :, columns].astype(f32) + recv[c, :, columns].astype(f32)).astype(bf16)
            moved = jnp.dot(gather_ref[...], summed, preferred_element_type=f32)
            outbox[c, :, :, columns] = moved.reshape(segments, CAP, PAIR).astype(bf16)
            square = moved * moved
            acc[...] += square[:, :HD] + square[:, HD:]
            return carry

        lax.fori_loop(0, step // PAIR, strip, 0)
        inbox[c, pl.ds(me, 1)] = outbox[c, pl.ds(me, 1)]

    def early_piece(c, carry):
        reduce_piece(c)
        send_piece(c)
        return carry

    lax.fori_loop(0, early, early_piece, 0)

    def late_piece(c, carry):
        reduce_piece(c)
        return carry

    lax.fori_loop(early, pieces, late_piece, 0)

    lane = lax.broadcasted_iota(jnp.int32, (CAP, HD), 1)
    diagonal = lane == lax.broadcasted_iota(jnp.int32, (CAP, HD), 0)

    def half_rows(i, carry):
        for u in range(8):
            s = i * 8 + u
            tile = acc[pl.ds(pl.multiple_of(s * CAP, CAP), CAP), :]
            column = jnp.sum(tile, axis=1, keepdims=True)
            half[s] = jnp.sum(jnp.where(diagonal, column, 0.0), axis=0, keepdims=True)
        return carry

    lax.fori_loop(0, segments // 8, half_rows, 0)
    halves = pltpu.make_async_remote_copy(
        src_ref=half, dst_ref=half_in, send_sem=hsend_sem, recv_sem=hrecv_sem,
        device_id=(me, other), device_id_type=MESH,
    )
    halves.start()

    arriving = dest_ref[...] == me
    ahead = jnp.dot(arriving.astype(f32).astype(bf16), before_ref[...], preferred_element_type=f32)
    key_ref[...] = jnp.where(arriving, ahead, -1.0)
    halves.wait()
    total[...] = half[...] + half_in[...]
    for offset in order:
        there = peer(offset)
        pltpu.make_async_remote_copy(
            src_ref=total.at[there], dst_ref=total_in.at[me], send_sem=tsend_sem, recv_sem=trecv_sem,
            device_id=(there, tp), device_id_type=MESH,
        ).start()
    total_in[pl.ds(me, 1)] = total[pl.ds(me, 1)]

    def late_send(c, carry):
        send_piece(c)
        return carry

    lax.fori_loop(early, pieces, late_send, 0)

    place = lax.broadcasted_iota(jnp.int32, (CAP, rows), 0).astype(f32)

    def columns_of(i, carry):
        for u in range(8):
            s = i * 8 + u
            found = key_ref[pl.ds(s, 1), :] == place
            at = pl.ds(pl.multiple_of(s * CAP, CAP), CAP)
            p = jnp.sum(jnp.where(found, pos_ref[pl.ds(s, 1), :].astype(f32), 0.0), axis=1, keepdims=True)
            posb[at, :] = jnp.broadcast_to(p, (CAP, HD))
            q = jnp.sum(jnp.where(found, slot_ref[pl.ds(s, 1), :].astype(f32), 0.0), axis=1, keepdims=True)
            slotb[at, :] = jnp.broadcast_to(q, (CAP, HD))
        return carry

    lax.fori_loop(0, segments // 8, columns_of, 0)

    row_in = lax.broadcasted_iota(jnp.int32, (BLOCK, BLOCK), 0)
    column_in = lax.broadcasted_iota(jnp.int32, (BLOCK, BLOCK), 1)
    same = (row_in // CAP) == (column_in // CAP)
    on_diagonal = row_in == column_in
    slots = lax.broadcasted_iota(jnp.int32, (rows, BLOCK), 0).astype(f32)
    half_sign = jnp.where(lax.broadcasted_iota(jnp.int32, (1, HD), 1) < HD // 2, -1.0, 1.0)

    def tables(b, carry):
        at = pl.ds(pl.multiple_of(b * BLOCK, BLOCK), BLOCK)
        p = posb[at, :]
        across = jnp.sum(jnp.where(on_diagonal, p, 0.0), axis=0, keepdims=True)
        bias_ref[at, :] = jnp.where(same & (across <= p), 0.0, -1e30)
        goes = jnp.sum(jnp.where(on_diagonal, slotb[at, :], 0.0), axis=0, keepdims=True)
        scatter_ref[:, at] = (slots == goes).astype(f32).astype(bf16)
        angle = p * freq_ref[...]
        cos_ref[at, :] = jnp.cos(angle)
        sin_ref[at, :] = jnp.sin(angle) * half_sign
        return carry

    lax.fori_loop(0, rows // BLOCK, tables, 0)
    scale_ref[0:1, :] = qscale_ref[...] * (math.log2(math.e) / math.sqrt(HD))
    scale_ref[1:2, :] = kscale_ref[...]

    every = pl.ds(0, segments - 1)
    pltpu.make_async_copy(total_in.at[every], total_in.at[every], trecv_sem).wait()
    whole = 1.0 / (2 * width)

    def inverse_rows(i, carry):
        for u in range(8):
            s = i * 8 + u
            column = jnp.sum(jnp.where(diagonal, total_in[s], 0.0), axis=1, keepdims=True)
            at = pl.ds(pl.multiple_of(s * CAP, CAP), CAP)
            inv_ref[at, :] = jnp.broadcast_to(lax.rsqrt(column * whole + EPS), (CAP, HD))
        return carry

    lax.fori_loop(0, segments // 8, inverse_rows, 0)

    ones = jnp.ones((BLOCK, HD), bf16)

    def out_copy(c):
        columns = pl.ds(pl.multiple_of(c * step, HD), step)
        return pltpu.make_async_copy(result.at[c], out_ref.at[:, columns], out_sem.at[c])

    def attend_piece(c, carry):
        pltpu.make_async_copy(inbox.at[c, every], inbox.at[c, every], recv_sem.at[c]).wait()

        def two_heads(i, carry):
            for u in range(2):
                local = pl.ds(pl.multiple_of(i * PAIR + u * HD, HD), HD)
                feature = pl.ds(pl.multiple_of(c * step + i * PAIR + u * HD, HD), HD)
                qs = scale_ref[0:1, feature]
                ks = scale_ref[1:2, feature]
                qr = pltpu.roll(qs, HD // 2, 1)
                kr = pltpu.roll(ks, HD // 2, 1)
                for b in range(rows // BLOCK):
                    at = pl.ds(b * BLOCK, BLOCK)
                    groups = pl.ds(b * (BLOCK // CAP), BLOCK // CAP)
                    x = inbox[c, groups, :, local].astype(f32).reshape(BLOCK, HD)
                    normed = x * inv_ref[at, :]
                    value = normed.astype(bf16)
                    straight = normed * cos_ref[at, :]
                    crossed = pltpu.roll(normed, HD // 2, 1) * sin_ref[at, :]
                    query = (straight * qs + crossed * qr).astype(bf16)
                    keys = (straight * ks + crossed * kr).astype(bf16)
                    scores = lax.dot_general(
                        query, keys, (((1,), (1,)), ((), ())), preferred_element_type=f32
                    ) + bias_ref[at, :]
                    top = jnp.max(scores, axis=1, keepdims=True)
                    weights = jnp.exp2(scores - top).astype(bf16)
                    both = jnp.dot(
                        weights, jnp.concatenate([value, ones], axis=1), preferred_element_type=f32
                    )
                    att_ref[at, u * HD:(u + 1) * HD] = (both[:, :HD] / both[:, HD:]).astype(bf16)
            placed = jnp.dot(scatter_ref[...], att_ref[...], preferred_element_type=f32)
            result[c, :, pl.ds(pl.multiple_of(i * PAIR, PAIR), PAIR)] = placed.astype(bf16)
            return carry

        lax.fori_loop(0, step // PAIR, two_heads, 0)
        out_copy(c).start()
        return carry

    lax.fori_loop(0, pieces, attend_piece, 0)

    for c in range(pieces):
        exchange(c).wait_send()
        out_copy(c).wait()
    sent = outbox.at[:, every]
    pltpu.make_async_copy(sent, sent, send_sem).wait()
    pltpu.make_async_copy(total.at[every], total.at[every], tsend_sem).wait()


def local(pieces, early, partials, kept_positions, destination, slot_index, query_scale, key_scale):
    f32, bf16 = jnp.float32, jnp.bfloat16
    rows, full = partials.shape[2:]
    width = full // 2
    step = width // pieces
    segments = destination.shape[0]
    side = round(segments ** (1 / 3))
    freq = np.exp(np.arange(HD // 2, dtype=np.float32) * np.float32(-2.0 * math.log(THETA) / HD))
    freq = jnp.asarray(np.concatenate([freq, freq])[None, :].astype(np.float32))
    vmem = pl.BlockSpec(memory_space=pltpu.VMEM)
    sem = pltpu.SemaphoreType.DMA
    return pl.pallas_call(
        functools.partial(kernel, side, rows, width, pieces, early),
        out_shape=jax.ShapeDtypeStruct((rows, width), bf16),
        in_specs=[pl.BlockSpec(memory_space=pl.ANY)] + [vmem] * 6,
        out_specs=pl.BlockSpec(memory_space=pl.ANY),
        scratch_shapes=[
            pltpu.VMEM((pieces, rows, step), bf16),
            pltpu.VMEM((pieces, rows, step), bf16),
            pltpu.VMEM((pieces, segments, CAP, step), bf16),
            pltpu.VMEM((pieces, segments, CAP, step), bf16),
            pltpu.VMEM((pieces, rows, step), bf16),
            pltpu.VMEM((rows, rows), bf16),
            pltpu.VMEM((rows, rows), bf16),
            pltpu.VMEM((rows, rows), bf16),
            pltpu.VMEM((segments, rows), f32),
            pltpu.VMEM((rows, HD), f32),
            pltpu.VMEM((rows, HD), f32),
            pltpu.VMEM((rows, HD), f32),
            pltpu.VMEM((rows, HD), f32),
            pltpu.VMEM((rows, BLOCK), f32),
            pltpu.VMEM((rows, HD), f32),
            pltpu.VMEM((segments, 1, HD), f32),
            pltpu.VMEM((segments, 1, HD), f32),
            pltpu.VMEM((segments, 1, HD), f32),
            pltpu.VMEM((segments, 1, HD), f32),
            pltpu.VMEM((rows, HD), f32),
            pltpu.VMEM((rows, PAIR), bf16),
            pltpu.VMEM((8, width), f32),
            sem((pieces,)), sem((pieces,)), sem((pieces,)),
            sem, sem((pieces,)),
            sem, sem, sem, sem,
            sem((pieces,)),
        ],
        compiler_params=pltpu.CompilerParams(
            collective_id=0, has_side_effects=True, vmem_limit_bytes=40 * 2**20
        ),
        name="handoff",
    )(
        partials.reshape(rows, full), kept_positions, destination, slot_index,
        query_scale[None, :], key_scale[None, :], freq,
    )


def solution(mesh):
    in_specs = (P("section", "tp", None, None), P(), P(), P(), P("tp"), P("tp"))
    return jax.shard_map(
        functools.partial(local, 4, 2), mesh=mesh, in_specs=in_specs,
        out_specs=P("section", "tp"), check_vma=False,
    )
```

time: 343 us -> 94.2 us (0.27)
  other arithmetic: 104 us -> 0 us
  local copies, waits for them, and re-layouts: 99 us -> 10.2 us
  Pallas kernels: 0 us -> 83.7 us
  waiting for transfers between devices: 76.7 us -> 0 us
  matrix products: 34.4 us -> 0 us
  between operations: 13.5 us -> 0.02 us
  starting transfers between devices: 10.6 us -> 0 us
  blocking collectives: 3.98 us -> 0 us
    pallas_call x0 -> x1, Pallas kernels: none -> 83.7 us  [local(): pl.pallas_call(functools.partial(kernel, side, rows, width, pieces, early...]
    psum x1 -> x0, waiting for transfers between devices: 47.1 us -> none  [local(): total = lax.psum(terms, 'tp').astype(jnp.float32)]
    dot_general x2 -> x0, matrix products: 34.4 us -> none  [the longest x1 19 us: attend(): jnp.einsum('qhd,khd->hqk', query, keys, preferred_element_type=jnp.float32)]
    sub x1 -> x0, other arithmetic: 34.3 us -> none  [attend(): expd = jnp.exp(scores - top)]
    all_to_all x1 -> x0, waiting for transfers between devices: 28.9 us -> none  [local(): lax.all_to_all(outbox, 'section', split_axis=0, concat_axis=0, tiled=True)]
    reduce_sum x4 -> x0, other arithmetic: 26.9 us -> none  [the longest x1 23.2 us: local(): packed_pos = jnp.sum(pick * kept_positions[:, :, None], (0, 1))]
    gather x2 -> x0, local copies, waits for them, and re-layouts: 22.6 us -> none  [the longest x1 11.3 us: local(): packed = jnp.take(inbox, inbox_row, axis=0)]
    another operation x6 -> x0, other arithmetic: 21.8 us -> none
  transfers between devices with their start and end apart: 2 -> 0, of which waited for: 2 -> 0; matrix products, arithmetic and copies ran while one was open for 8% -> 0% of each run, Pallas kernels for 0% -> 0%
where the time goes in v1:
time: 94.2 us; the launch traced here: 93.9 us
  Pallas kernels  83.7 us (89%)
  local copies, waits for them, and re-layouts  10.2 us (11%)
    pallas_call x1, Pallas kernels, local(): pl.pallas_call(functools.partial(kernel, side, rows, width, pieces, early...  83.7 us
    unnamed x15, local copies, waits for them, and re-layouts  10.2 us

profile of v1, /device:TPU:1, one launch (start us, length us, event | category | flops | bytes accessed | tf_op | source)
XLA Modules:
  0.0 93.9 jit_solution(10732187649428131927)
XLA Ops:
  0.0 0.0 copy-start
  0.0 3.4 %copy-done = bf16[1,1,512,8192]{3,2,1,0:T(8,128)(2,1)S(1)} copy-done((bf16[1,1,512,8192]{3,2,1,0:T(8,128)(2,1)S(1)}, bf16[1,1,512,8192]{3,2,1,0:T(8,128)(2,1)}, u32[]{:S(2)}) %copy-start) | copy-done | bytes 8388632
  3.4 0.0 copy-start.1
  3.4 0.9 copy-done.1
  4.3 0.0 copy-start.2
  4.3 0.9 copy-done.2
  5.2 0.0 copy-start.3
  5.2 0.9 copy-done.3
  6.1 0.0 copy-start.4
  6.1 0.7 copy-done.4
  6.8 0.0 copy-start.5
  6.8 0.7 copy-done.5
  7.5 0.0 copy-start.6
  7.5 0.7 copy-done.6
  8.2 83.7 %handoff.1 = bf16[512,4096]{1,0:T(8,128)(2,1)S(1)} custom-call(bf16[512,8192]{1,0:T(8,128)(2,1)S(1)} %bitcast.3, s32[64,512]{1,0:T(8,128)S(1)} %copy-done.1, s32[64,512]{1,0:T(8,128)S(1)} %copy-done.2, s32[64,512]{1,0:T(8,128)S(1)} %copy-done.3, f32[1,4096]{1,0:T(1,128)S(1)} %bitcast.4, f32[1,4096]{1,0:T(1,128)S(1)} %bitcast.5, f32[1,128]{1,0:T(1,128)S(1)} %copy-done.6), custom_call_target="tpu_custom_call" | custom-call | tf_op jit(solution)/shard_map/handoff/pallas_call | solution.py:299
  91.9 2.0 %copy.9 = bf16[512,4096]{1,0:T(8,128)(2,1)} copy(bf16[512,4096]{1,0:T(8,128)(2,1)S(1)} %handoff.1) | data formatting | bytes 8388608
Async XLA Ops:
  0.0 3.4 %copy-start = (bf16[1,1,512,8192]{3,2,1,0:T(8,128)(2,1)S(1)}, bf16[1,1,512,8192]{3,2,1,0:T(8,128)(2,1)}, u32[]{:S(2)}) copy-start(bf16[1,1,512,8192]{3,2,1,0:T(8,128)(2,1)} %param.7) | copy-start | bytes 25165828
  3.4 0.9 copy-start.1
  4.3 0.9 copy-start.2
  5.2 0.9 copy-start.3
  6.1 0.7 copy-start.4
  6.8 0.7 copy-start.5
  7.5 0.7 copy-start.6

commit v2 on v1

v2 whole, which is shorter than its diff:
```python
import functools
import math

import jax
import jax.numpy as jnp
import numpy as np
from jax import lax
from jax.experimental import pallas as pl
from jax.experimental.pallas import tpu as pltpu
from jax.sharding import PartitionSpec as P

HD = 128
CAP = 8
EPS = 1e-05
THETA = 500000.0
BLOCK = 128
HEADS = 4
UNIT = HEADS * HD
MESH = pl.DeviceIdType.MESH


def link_load(offset):
    load = [0] * 6
    for axis, step in enumerate(offset):
        if step in (1, 2):
            load[2 * axis] += 1
        if step in (2, 3):
            load[2 * axis + 1] += 1
    return load


def offset_order(side):
    rest = [(a, b, c) for a in range(side) for b in range(side) for c in range(side)][1:]
    total = [0] * 6
    order = []
    while rest:
        def cost(offset):
            load = link_load(offset)
            after = [t + l for t, l in zip(total, load)]
            mean = sum(after) / 6
            return max(after) - min(after), sum((a - mean) ** 2 for a in after), -sum(load)

        best = min(rest, key=cost)
        rest.remove(best)
        total = [t + l for t, l in zip(total, link_load(best))]
        order.append(best)
    return order


def kernel(
    side, rows, width,
    part_ref, pos_in, dest_in, slot_in, qscale_in, kscale_in, freq_in,
    out_ref,
    dest_ref, pos_ref, slot_ref, qscale_ref, kscale_ref, freq_ref,
    own, recv, outbox, inbox, before_ref, gather_ref, scatter_ref, key_ref,
    posb, slotb, cos_ref, sin_ref, bias_ref, acc, half, half_in, total, total_in, inv_ref, att_ref, scale_ref,
    own_sem, xsend_sem, xrecv_sem, send_sem, recv_sem, hsend_sem, hrecv_sem, tsend_sem, trecv_sem, load_sem,
):
    f32, bf16 = jnp.float32, jnp.bfloat16
    segments = side ** 3
    units = width // UNIT
    me = lax.axis_index("section")
    tp = lax.axis_index("tp")
    other = 1 - tp
    here = (me // (side * side), (me // side) % side, me % side)
    order = offset_order(side)

    def peer(offset):
        at = [lax.rem(h + o, side) for h, o in zip(here, offset)]
        return (at[0] * side + at[1]) * side + at[2]

    barrier = pltpu.get_barrier_semaphore()

    def own_copy(u):
        columns = pl.ds(pl.multiple_of(tp * width + u * UNIT, UNIT), UNIT)
        return pltpu.make_async_copy(part_ref.at[:, columns], own.at[u], own_sem.at[u])

    def exchange(u):
        columns = pl.ds(pl.multiple_of(other * width + u * UNIT, UNIT), UNIT)
        return pltpu.make_async_remote_copy(
            src_ref=part_ref.at[:, columns], dst_ref=recv.at[u],
            send_sem=xsend_sem.at[u], recv_sem=xrecv_sem.at[u],
            device_id=(me, other), device_id_type=MESH,
        )

    pl.semaphore_signal(barrier, inc=1, device_id=(me, other), device_id_type=MESH)
    for offset in order:
        pl.semaphore_signal(barrier, inc=1, device_id=(peer(offset), tp), device_id_type=MESH)
    loads = [
        pltpu.make_async_copy(source, place, load_sem.at[i])
        for i, (source, place) in enumerate((
            (dest_in, dest_ref), (pos_in, pos_ref), (slot_in, slot_ref),
            (qscale_in, qscale_ref), (kscale_in, kscale_ref), (freq_in, freq_ref),
        ))
    ]
    for load in loads:
        load.start()
    for u in range(units):
        own_copy(u).start()

    before_ref[...] = (
        lax.broadcasted_iota(jnp.int32, (rows, rows), 0) < lax.broadcasted_iota(jnp.int32, (rows, rows), 1)
    ).astype(f32).astype(bf16)
    loads[0].wait()
    mine = dest_ref[pl.ds(me, 1), :]
    member = mine == lax.broadcasted_iota(jnp.int32, (segments, rows), 0)
    ahead = jnp.dot(member.astype(f32).astype(bf16), before_ref[...], preferred_element_type=f32)
    rank = jnp.sum(jnp.where(member, ahead, 0.0), axis=0, keepdims=True)
    target = mine * CAP + rank.astype(jnp.int32)
    gather_ref[...] = (
        lax.broadcasted_iota(jnp.int32, (rows, rows), 0) == target
    ).astype(f32).astype(bf16)
    acc[...] = jnp.zeros_like(acc)

    pl.semaphore_wait(barrier, segments)
    for u in range(2):
        exchange(u).start()

    def send(first, count, piece):
        for offset in order:
            there = peer(offset)
            pltpu.make_async_remote_copy(
                src_ref=outbox.at[pl.ds(first, count), there], dst_ref=inbox.at[pl.ds(first, count), me],
                send_sem=send_sem, recv_sem=recv_sem.at[piece],
                device_id=(there, tp), device_id_type=MESH,
            ).start()

    def reduce_unit(u, carry):
        own_copy(u).wait()
        exchange(u).wait_recv()

        @pl.when(u + 2 < units)
        def _():
            exchange(u + 2).start()

        for i in range(HEADS // 2):
            columns = slice(2 * i * HD, 2 * (i + 1) * HD)
            summed = (own[u, :, columns].astype(f32) + recv[u, :, columns].astype(f32)).astype(bf16)
            moved = jnp.dot(gather_ref[...], summed, preferred_element_type=f32)
            outbox[u, :, :, columns] = moved.reshape(segments, CAP, 2 * HD).astype(bf16)
            square = moved * moved
            acc[...] += square[:, :HD] + square[:, HD:]
        inbox[u, pl.ds(me, 1)] = outbox[u, pl.ds(me, 1)]
        return carry

    lax.fori_loop(0, 1, reduce_unit, 0)
    send(0, 1, 0)
    lax.fori_loop(1, 3, reduce_unit, 0)
    send(1, 2, 1)
    lax.fori_loop(3, units, reduce_unit, 0)

    lane = lax.broadcasted_iota(jnp.int32, (CAP, HD), 1)
    diagonal = lane == lax.broadcasted_iota(jnp.int32, (CAP, HD), 0)

    def half_rows(i, carry):
        for u in range(8):
            s = i * 8 + u
            tile = acc[pl.ds(pl.multiple_of(s * CAP, CAP), CAP), :]
            column = jnp.sum(tile, axis=1, keepdims=True)
            half[s] = jnp.sum(jnp.where(diagonal, column, 0.0), axis=0, keepdims=True)
        return carry

    lax.fori_loop(0, segments // 8, half_rows, 0)
    halves = pltpu.make_async_remote_copy(
        src_ref=half, dst_ref=half_in, send_sem=hsend_sem, recv_sem=hrecv_sem,
        device_id=(me, other), device_id_type=MESH,
    )
    halves.start()

    arriving = dest_ref[...] == me
    ahead = jnp.dot(arriving.astype(f32).astype(bf16), before_ref[...], preferred_element_type=f32)
    key_ref[...] = jnp.where(arriving, ahead, -1.0)
    halves.wait()
    total[...] = half[...] + half_in[...]
    for offset in order:
        there = peer(offset)
        pltpu.make_async_remote_copy(
            src_ref=total.at[there], dst_ref=total_in.at[me], send_sem=tsend_sem, recv_sem=trecv_sem,
            device_id=(there, tp), device_id_type=MESH,
        ).start()
    total_in[pl.ds(me, 1)] = total[pl.ds(me, 1)]

    def send_middle(p, carry):
        send(2 * p - 1, 2, p)
        return carry

    lax.fori_loop(2, units // 2, send_middle, 0)
    send(units - 1, 1, units // 2)

    for load in loads[1:]:
        load.wait()
    place = lax.broadcasted_iota(jnp.int32, (CAP, rows), 0).astype(f32)

    def columns_of(i, carry):
        for u in range(8):
            s = i * 8 + u
            found = key_ref[pl.ds(s, 1), :] == place
            at = pl.ds(pl.multiple_of(s * CAP, CAP), CAP)
            p = jnp.sum(jnp.where(found, pos_ref[pl.ds(s, 1), :].astype(f32), 0.0), axis=1, keepdims=True)
            posb[at, :] = jnp.broadcast_to(p, (CAP, HD))
            q = jnp.sum(jnp.where(found, slot_ref[pl.ds(s, 1), :].astype(f32), 0.0), axis=1, keepdims=True)
            slotb[at, :] = jnp.broadcast_to(q, (CAP, HD))
        return carry

    lax.fori_loop(0, segments // 8, columns_of, 0)

    row_in = lax.broadcasted_iota(jnp.int32, (BLOCK, BLOCK), 0)
    column_in = lax.broadcasted_iota(jnp.int32, (BLOCK, BLOCK), 1)
    same = (row_in // CAP) == (column_in // CAP)
    on_diagonal = row_in == column_in
    slots = lax.broadcasted_iota(jnp.int32, (rows, BLOCK), 0).astype(f32)
    half_sign = jnp.where(lax.broadcasted_iota(jnp.int32, (1, HD), 1) < HD // 2, -1.0, 1.0)

    def tables(b, carry):
        at = pl.ds(pl.multiple_of(b * BLOCK, BLOCK), BLOCK)
        p = posb[at, :]
        across = jnp.sum(jnp.where(on_diagonal, p, 0.0), axis=0, keepdims=True)
        bias_ref[at, :] = jnp.where(same & (across <= p), 0.0, -1e30)
        goes = jnp.sum(jnp.where(on_diagonal, slotb[at, :], 0.0), axis=0, keepdims=True)
        scatter_ref[:, at] = (slots == goes).astype(f32).astype(bf16)
        angle = p * freq_ref[...]
        cos_ref[at, :] = jnp.cos(angle)
        sin_ref[at, :] = jnp.sin(angle) * half_sign
        return carry

    lax.fori_loop(0, rows // BLOCK, tables, 0)
    scale_ref[0:1, :] = qscale_ref[...] * (math.log2(math.e) / math.sqrt(HD))
    scale_ref[1:2, :] = kscale_ref[...]

    every = pl.ds(0, segments - 1)
    pltpu.make_async_copy(total_in.at[every], total_in.at[every], trecv_sem).wait()
    whole = 1.0 / (2 * width)

    def inverse_rows(i, carry):
        for u in range(8):
            s = i * 8 + u
            column = jnp.sum(jnp.where(diagonal, total_in[s], 0.0), axis=1, keepdims=True)
            at = pl.ds(pl.multiple_of(s * CAP, CAP), CAP)
            inv_ref[at, :] = jnp.broadcast_to(lax.rsqrt(column * whole + EPS), (CAP, HD))
        return carry

    lax.fori_loop(0, segments // 8, inverse_rows, 0)

    ones = jnp.ones((BLOCK, HD), bf16)

    def arrived(first, count, piece):
        at = inbox.at[pl.ds(first, count), every]
        pltpu.make_async_copy(at, at, recv_sem.at[piece]).wait()

    def attend_unit(unit, carry):
        @pl.when(unit == 0)
        def _():
            arrived(0, 1, 0)

        @pl.when((unit % 2 == 1) & (unit < units - 1))
        def _():
            arrived(unit, 2, (unit + 1) // 2)

        @pl.when(unit == units - 1)
        def _():
            arrived(units - 1, 1, units // 2)

        tiles = []
        for h in range(HEADS):
            local = slice(h * HD, (h + 1) * HD)
            feature = pl.ds(pl.multiple_of(unit * UNIT + h * HD, HD), HD)
            qs = scale_ref[0:1, feature]
            ks = scale_ref[1:2, feature]
            qr = pltpu.roll(qs, HD // 2, 1)
            kr = pltpu.roll(ks, HD // 2, 1)
            for b in range(rows // BLOCK):
                at = slice(b * BLOCK, (b + 1) * BLOCK)
                groups = slice(b * (BLOCK // CAP), (b + 1) * (BLOCK // CAP))
                x = inbox[unit, groups, :, local].astype(f32).reshape(BLOCK, HD)
                normed = x * inv_ref[at, :]
                straight = normed * cos_ref[at, :]
                crossed = pltpu.roll(normed, HD // 2, 1) * sin_ref[at, :]
                query = (straight * qs + crossed * qr).astype(bf16)
                keys = (straight * ks + crossed * kr).astype(bf16)
                tiles.append((at, local, query, keys, normed.astype(bf16)))
        scores = [
            lax.dot_general(query, keys, (((1,), (1,)), ((), ())), preferred_element_type=f32)
            for _, _, query, keys, _ in tiles
        ]
        weights = []
        for (at, *_), score in zip(tiles, scores):
            score = score + bias_ref[at, :]
            top = jnp.max(score, axis=1, keepdims=True)
            weights.append(jnp.exp2(score - top).astype(bf16))
        sums = [
            jnp.dot(weight, jnp.concatenate([value, ones], axis=1), preferred_element_type=f32)
            for (*_, value), weight in zip(tiles, weights)
        ]
        for (at, local, *_), both in zip(tiles, sums):
            att_ref[at, local] = (both[:, :HD] / both[:, HD:]).astype(bf16)
        placed = jnp.dot(scatter_ref[...], att_ref[...], preferred_element_type=f32)
        out_ref[:, pl.ds(pl.multiple_of(unit * UNIT, UNIT), UNIT)] = placed.astype(bf16)
        return carry

    lax.fori_loop(0, units, attend_unit, 0)

    for u in range(units):
        exchange(u).wait_send()
    sent = outbox.at[:, every]
    pltpu.make_async_copy(sent, sent, send_sem).wait()
    pltpu.make_async_copy(total.at[every], total.at[every], tsend_sem).wait()


def local(partials, kept_positions, destination, slot_index, query_scale, key_scale):
    f32, bf16 = jnp.float32, jnp.bfloat16
    rows, full = partials.shape[2:]
    width = full // 2
    units = width // UNIT
    segments = destination.shape[0]
    side = round(segments ** (1 / 3))
    freq = np.exp(np.arange(HD // 2, dtype=np.float32) * np.float32(-2.0 * math.log(THETA) / HD))
    freq = jnp.asarray(np.concatenate([freq, freq])[None, :].astype(np.float32))
    vmem = pl.BlockSpec(memory_space=pltpu.VMEM)
    sem = pltpu.SemaphoreType.DMA
    return pl.pallas_call(
        functools.partial(kernel, side, rows, width),
        out_shape=pltpu.VMEM((rows, width), bf16),
        in_specs=[pl.BlockSpec(memory_space=pltpu.HBM)] * 7,
        out_specs=vmem,
        scratch_shapes=[
            pltpu.VMEM(destination.shape, jnp.int32),
            pltpu.VMEM(destination.shape, jnp.int32),
            pltpu.VMEM(destination.shape, jnp.int32),
            pltpu.VMEM((1, width), f32),
            pltpu.VMEM((1, width), f32),
            pltpu.VMEM((1, HD), f32),
            pltpu.VMEM((units, rows, UNIT), bf16),
            pltpu.VMEM((units, rows, UNIT), bf16),
            pltpu.VMEM((units, segments, CAP, UNIT), bf16),
            pltpu.VMEM((units, segments, CAP, UNIT), bf16),
            pltpu.VMEM((rows, rows), bf16),
            pltpu.VMEM((rows, rows), bf16),
            pltpu.VMEM((rows, rows), bf16),
            pltpu.VMEM((segments, rows), f32),
            pltpu.VMEM((rows, HD), f32),
            pltpu.VMEM((rows, HD), f32),
            pltpu.VMEM((rows, HD), f32),
            pltpu.VMEM((rows, HD), f32),
            pltpu.VMEM((rows, BLOCK), f32),
            pltpu.VMEM((rows, HD), f32),
            pltpu.VMEM((segments, 1, HD), f32),
            pltpu.VMEM((segments, 1, HD), f32),
            pltpu.VMEM((segments, 1, HD), f32),
            pltpu.VMEM((segments, 1, HD), f32),
            pltpu.VMEM((rows, HD), f32),
            pltpu.VMEM((rows, UNIT), bf16),
            pltpu.VMEM((8, width), f32),
            sem((units,)), sem((units,)), sem((units,)),
            sem, sem((units // 2 + 1,)),
            sem, sem, sem, sem,
            sem((6,)),
        ],
        compiler_params=pltpu.CompilerParams(
            collective_id=0, has_side_effects=True, vmem_limit_bytes=40 * 2**20
        ),
        name="handoff",
    )(*(
        pltpu.with_memory_space_constraint(array, pltpu.HBM)
        for array in (
            partials.reshape(rows, full), kept_positions, destination, slot_index,
            query_scale[None, :], key_scale[None, :], freq,
        )
    ))


def solution(mesh):
    in_specs = (P("section", "tp", None, None), P(), P(), P(), P("tp"), P("tp"))
    return jax.shard_map(
        local, mesh=mesh, in_specs=in_specs,
        out_specs=P("section", "tp"), check_vma=False,
    )
```

time: 94.2 us -> 64.7 us (0.69)
  Pallas kernels: 83.7 us -> 62.6 us
  local copies, waits for them, and re-layouts: 10.2 us -> 2.02 us
    pallas_call x1, Pallas kernels: 83.7 us -> 62.6 us  [local(): pl.pallas_call(functools.partial(kernel, side, rows, width), out_shape=pl...]
    unnamed x15 -> x1, local copies, waits for them, and re-layouts: 10.2 us -> 2.02 us
where the time goes in v2:
time: 64.7 us; the launch traced here: 64.6 us
  Pallas kernels  62.6 us (97%)
  local copies, waits for them, and re-layouts  2.02 us (3%)
    pallas_call x1, Pallas kernels, local(): pl.pallas_call(functools.partial(kernel, side, rows, width), out_shape=pl...  62.6 us
    unnamed x1, local copies, waits for them, and re-layouts  2.02 us

profile of v2, /device:TPU:1, one launch (start us, length us, event | category | flops | bytes accessed | tf_op | source)
XLA Modules:
  0.0 64.6 jit_solution(7748896930638954217)
XLA Ops:
  0.0 62.6 %handoff.1 = bf16[512,4096]{1,0:T(8,128)(2,1)S(1)} custom-call(bf16[512,8192]{1,0:T(8,128)(2,1)} %bitcast.3, s32[64,512]{1,0:T(8,128)} %pos_in.1, s32[64,512]{1,0:T(8,128)} %dest_in.1, s32[64,512]{1,0:T(8,128)} %slot_in.1, f32[1,4096]{1,0:T(1,128)} %bitcast.4, f32[1,4096]{1,0:T(1,128)} %bitcast.5, f32[1,128]{1,0:T(1,128)} %constant.2.clone.freq_in), custom_call_target="tpu_custom_call" | custom-call | tf_op jit(solution)/shard_map/handoff/pallas_call | solution.py:320
  62.6 2.0 %copy.9 = bf16[512,4096]{1,0:T(8,128)(2,1)} copy(bf16[512,4096]{1,0:T(8,128)(2,1)S(1)} %handoff.1) | data formatting | bytes 8388608

commit v3 on v2

v3 whole, which is shorter than its diff:
```python
import functools
import math

import jax
import jax.numpy as jnp
import numpy as np
from jax import lax
from jax.experimental import pallas as pl
from jax.experimental.pallas import tpu as pltpu
from jax.sharding import PartitionSpec as P

HD = 128
CAP = 8
EPS = 1e-05
THETA = 500000.0
BLOCK = 128
HEADS = 4
UNIT = HEADS * HD
STRIP = UNIT // 2
MESH = pl.DeviceIdType.MESH


def attend(load, store, inv_ref, cos_ref, sin_ref, bias_ref, scale_ref, first):
    f32, bf16 = jnp.float32, jnp.bfloat16
    rows = inv_ref.shape[0]
    ones = jnp.ones((BLOCK, HD), bf16)
    tiles = []
    for h in range(HEADS):
        local = slice(h * HD, (h + 1) * HD)
        feature = pl.ds(pl.multiple_of(first + h * HD, HD), HD)
        qs = scale_ref[0:1, feature]
        ks = scale_ref[1:2, feature]
        qr = pltpu.roll(qs, HD // 2, 1)
        kr = pltpu.roll(ks, HD // 2, 1)
        for b in range(rows // BLOCK):
            at = slice(b * BLOCK, (b + 1) * BLOCK)
            groups = slice(b * (BLOCK // CAP), (b + 1) * (BLOCK // CAP))
            x = load(groups, local).astype(f32).reshape(BLOCK, HD)
            normed = x * inv_ref[at, :]
            straight = normed * cos_ref[at, :]
            crossed = pltpu.roll(normed, HD // 2, 1) * sin_ref[at, :]
            query = (straight * qs + crossed * qr).astype(bf16)
            keys = (straight * ks + crossed * kr).astype(bf16)
            tiles.append((at, groups, local, query, keys, normed.astype(bf16)))
    scores = [
        lax.dot_general(query, keys, (((1,), (1,)), ((), ())), preferred_element_type=f32)
        for _, _, _, query, keys, _ in tiles
    ]
    weights = []
    for (at, *_), score in zip(tiles, scores):
        score = score + bias_ref[at, :]
        top = jnp.max(score, axis=1, keepdims=True)
        weights.append(jnp.exp2(score - top).astype(bf16))
    sums = [
        jnp.dot(weight, jnp.concatenate([value, ones], axis=1), preferred_element_type=f32)
        for (*_, value), weight in zip(tiles, weights)
    ]
    for (at, groups, local, *_), both in zip(tiles, sums):
        store(at, groups, local, both[:, :HD] / both[:, HD:])


def link_load(offset):
    load = [0] * 6
    for axis, step in enumerate(offset):
        if step in (1, 2):
            load[2 * axis] += 1
        if step in (2, 3):
            load[2 * axis + 1] += 1
    return load


def offset_order(side):
    rest = [(a, b, c) for a in range(side) for b in range(side) for c in range(side)][1:]
    total = [0] * 6
    order = []
    while rest:
        def cost(offset):
            load = link_load(offset)
            after = [t + l for t, l in zip(total, load)]
            mean = sum(after) / 6
            return max(after) - min(after), sum((a - mean) ** 2 for a in after), -sum(load)

        best = min(rest, key=cost)
        rest.remove(best)
        total = [t + l for t, l in zip(total, link_load(best))]
        order.append(best)
    return order


def kernel(
    side, rows, width,
    part_ref, pos_in, dest_in, slot_in, qscale_in, kscale_in, freq_in,
    placed_ref, last_ref, scatter_ref,
    dest_ref, pos_ref, slot_ref, qscale_ref, kscale_ref, freq_ref,
    own, recv, outbox, inbox, before_ref, gather_ref, key_ref,
    inv_ref, cos_ref, sin_ref, bias_ref, scale_ref,
    posb, slotb, acc, half, half_in, total, total_in, att_ref,
    own_sem, xsend_sem, xrecv_sem, send_sem, recv_sem, hsend_sem, hrecv_sem, tsend_sem, trecv_sem, load_sem,
):
    f32, bf16 = jnp.float32, jnp.bfloat16
    segments = side ** 3
    units = width // UNIT
    me = lax.axis_index("section")
    tp = lax.axis_index("tp")
    other = 1 - tp
    strips = width // STRIP
    z, y, x = me // (side * side), lax.rem(me // side, side), lax.rem(me, side)

    order = offset_order(side)

    def each_peer(act):
        for offset in order:
            at = [lax.rem(h + o, side) for h, o in zip((z, y, x), offset)]
            act((at[0] * side + at[1]) * side + at[2])

    barrier = pltpu.get_barrier_semaphore()

    def own_copy(u):
        columns = pl.ds(pl.multiple_of(tp * width + u * STRIP, STRIP), STRIP)
        return pltpu.make_async_copy(part_ref.at[:, columns], own.at[u], own_sem.at[u])

    def exchange(u):
        columns = pl.ds(pl.multiple_of(other * width + u * STRIP, STRIP), STRIP)
        return pltpu.make_async_remote_copy(
            src_ref=part_ref.at[:, columns], dst_ref=recv.at[u],
            send_sem=xsend_sem.at[u], recv_sem=xrecv_sem.at[u],
            device_id=(me, other), device_id_type=MESH,
        )

    pl.semaphore_signal(barrier, inc=1, device_id=(me, other), device_id_type=MESH)
    each_peer(lambda there: pl.semaphore_signal(barrier, inc=1, device_id=(there, tp), device_id_type=MESH))
    loads = [
        pltpu.make_async_copy(source, place, load_sem.at[i])
        for i, (source, place) in enumerate((
            (dest_in, dest_ref), (pos_in, pos_ref), (slot_in, slot_ref),
            (qscale_in, qscale_ref), (kscale_in, kscale_ref), (freq_in, freq_ref),
        ))
    ]
    for load in loads:
        load.start()
    for u in range(strips):
        own_copy(u).start()

    before_ref[...] = (
        lax.broadcasted_iota(jnp.int32, (rows, rows), 0) < lax.broadcasted_iota(jnp.int32, (rows, rows), 1)
    ).astype(f32).astype(bf16)
    loads[0].wait()
    mine = dest_ref[pl.ds(me, 1), :]
    member = mine == lax.broadcasted_iota(jnp.int32, (segments, rows), 0)
    ahead = jnp.dot(member.astype(f32).astype(bf16), before_ref[...], preferred_element_type=f32)
    rank = jnp.sum(jnp.where(member, ahead, 0.0), axis=0, keepdims=True)
    target = mine * CAP + rank.astype(jnp.int32)
    gather_ref[...] = (
        lax.broadcasted_iota(jnp.int32, (rows, rows), 0) == target
    ).astype(f32).astype(bf16)
    acc[...] = jnp.zeros_like(acc)

    pl.semaphore_wait(barrier, segments)
    for u in range(2):
        exchange(u).start()

    def send(source, target, piece):
        def one(there):
            pltpu.make_async_remote_copy(
                src_ref=source(there), dst_ref=target, send_sem=send_sem, recv_sem=recv_sem.at[piece],
                device_id=(there, tp), device_id_type=MESH,
            ).start()

        each_peer(one)

    def send_half(i):
        columns = pl.ds(i * STRIP, STRIP)
        send(lambda there: outbox.at[0, there, :, columns], inbox.at[0, me, :, columns], i)

    def send_pair(p, carry):
        two = pl.ds(2 * p - 3, 2)
        send(lambda there: outbox.at[two, there], inbox.at[two, me], p)
        return carry

    def reduce_strip(u, carry):
        own_copy(u).wait()
        exchange(u).wait_recv()

        @pl.when(u + 2 < strips)
        def _():
            exchange(u + 2).start()

        unit = u // 2
        columns = pl.ds(pl.multiple_of(lax.rem(u, 2) * STRIP, STRIP), STRIP)
        summed = (own[u].astype(f32) + recv[u].astype(f32)).astype(bf16)
        moved = jnp.dot(gather_ref[...], summed, preferred_element_type=f32)
        outbox[unit, :, :, columns] = moved.reshape(segments, CAP, STRIP).astype(bf16)
        square = moved * moved
        acc[...] += square[:, :HD] + square[:, HD:]
        return carry

    lax.fori_loop(0, 1, reduce_strip, 0)
    send_half(0)
    lax.fori_loop(1, 2, reduce_strip, 0)
    send_half(1)
    lax.fori_loop(2, 6, reduce_strip, 0)
    send_pair(2, 0)
    lax.fori_loop(6, 10, reduce_strip, 0)
    send_pair(3,0)
    lax.fori_loop(10, strips, reduce_strip, 0)
    mine_too = pl.ds(me, 1)
    inbox[:, mine_too] = outbox[pl.ds(0, units - 1), mine_too]

    lane = lax.broadcasted_iota(jnp.int32, (CAP, HD), 1)
    diagonal = lane == lax.broadcasted_iota(jnp.int32, (CAP, HD), 0)

    def half_rows(i, carry):
        for u in range(8):
            s = i * 8 + u
            tile = acc[pl.ds(pl.multiple_of(s * CAP, CAP), CAP), :]
            column = jnp.sum(tile, axis=1, keepdims=True)
            half[s] = jnp.sum(jnp.where(diagonal, column, 0.0), axis=0, keepdims=True)
        return carry

    lax.fori_loop(0, segments // 8, half_rows, 0)
    halves = pltpu.make_async_remote_copy(
        src_ref=half, dst_ref=half_in, send_sem=hsend_sem, recv_sem=hrecv_sem,
        device_id=(me, other), device_id_type=MESH,
    )
    halves.start()

    arriving = dest_ref[...] == me
    ahead = jnp.dot(arriving.astype(f32).astype(bf16), before_ref[...], preferred_element_type=f32)
    key_ref[...] = jnp.where(arriving, ahead, -1.0)
    halves.wait()
    total[...] = half[...] + half_in[...]

    def send_total(there):
        pltpu.make_async_remote_copy(
            src_ref=total.at[there], dst_ref=total_in.at[me], send_sem=tsend_sem, recv_sem=trecv_sem,
            device_id=(there, tp), device_id_type=MESH,
        ).start()

    each_peer(send_total)
    total_in[pl.ds(me, 1)] = total[pl.ds(me, 1)]

    pairs = units // 2 + 1
    lax.fori_loop(4, pairs, send_pair, 0)

    for load in loads[1:]:
        load.wait()
    scale_ref[0:1, :] = qscale_ref[...] * (math.log2(math.e) / math.sqrt(HD))
    scale_ref[1:2, :] = kscale_ref[...]
    place = lax.broadcasted_iota(jnp.int32, (CAP, rows), 0).astype(f32)
    row_in = lax.broadcasted_iota(jnp.int32, (BLOCK, BLOCK), 0)
    column_in = lax.broadcasted_iota(jnp.int32, (BLOCK, BLOCK), 1)
    same = (row_in // CAP) == (column_in // CAP)
    on_diagonal = row_in == column_in
    half_sign = jnp.where(lax.broadcasted_iota(jnp.int32, (1, HD), 1) < HD // 2, -1.0, 1.0)
    whole = 1.0 / (2 * width)

    def spread(found, row):
        column = jnp.sum(jnp.where(found, row.astype(f32), 0.0), axis=1, keepdims=True)
        return jnp.broadcast_to(column, (CAP, HD))

    def tables(b, carry):
        at = pl.ds(pl.multiple_of(b * BLOCK, BLOCK), BLOCK)
        p = posb[at, :]
        across = jnp.sum(jnp.where(on_diagonal, p, 0.0), axis=0, keepdims=True)
        bias_ref[at, :] = jnp.where(same & (across <= p), 0.0, -1e30)
        angle = p * freq_ref[...]
        cos_ref[at, :] = jnp.cos(angle)
        sin_ref[at, :] = jnp.sin(angle) * half_sign
        return carry

    def inverse_rows(sums):
        def some(i, carry):
            for u in range(8):
                s = i * 8 + u
                column = jnp.sum(jnp.where(diagonal, sums[s], 0.0), axis=1, keepdims=True)
                at = pl.ds(pl.multiple_of(s * CAP, CAP), CAP)
                inv_ref[at, :] = jnp.broadcast_to(lax.rsqrt(column * whole + EPS), (CAP, HD))
            return carry

        lax.fori_loop(0, segments // 8, some, 0)

    leaving = target.astype(f32)
    leaving_pos = pos_ref[pl.ds(me, 1), :]

    def leaving_columns(i, carry):
        for u in range(8):
            s = i * 8 + u
            found = leaving == place + (s * CAP).astype(f32)
            posb[pl.ds(pl.multiple_of(s * CAP, CAP), CAP), :] = spread(found, leaving_pos)
        return carry

    lax.fori_loop(0, segments // 8, leaving_columns, 0)
    lax.fori_loop(0, rows // BLOCK, tables, 0)
    inverse_rows(total)
    last = units - 1

    def store_leaving(at, groups, local, value):
        outbox[last, groups, :, local] = value.reshape(BLOCK // CAP, CAP, HD).astype(bf16)

    attend(
        lambda groups, local: outbox[last, groups, :, local], store_leaving,
        inv_ref, cos_ref, sin_ref, bias_ref, scale_ref, last * UNIT,
    )
    send(lambda there: outbox.at[last, there], last_ref.at[me], pairs)
    last_ref[mine_too] = outbox[last, mine_too]

    def columns_of(i, carry):
        for u in range(8):
            s = i * 8 + u
            found = key_ref[pl.ds(s, 1), :] == place
            at = pl.ds(pl.multiple_of(s * CAP, CAP), CAP)
            posb[at, :] = spread(found, pos_ref[pl.ds(s, 1), :])
            slotb[at, :] = spread(found, slot_ref[pl.ds(s, 1), :])
        return carry

    lax.fori_loop(0, segments // 8, columns_of, 0)
    lax.fori_loop(0, rows // BLOCK, tables, 0)
    slots = lax.broadcasted_iota(jnp.int32, (rows, BLOCK), 0).astype(f32)

    def scatter_block(b, carry):
        at = pl.ds(pl.multiple_of(b * BLOCK, BLOCK), BLOCK)
        goes = jnp.sum(jnp.where(on_diagonal, slotb[at, :], 0.0), axis=0, keepdims=True)
        scatter_ref[:, at] = (slots == goes).astype(f32).astype(bf16)
        return carry

    lax.fori_loop(0, rows // BLOCK, scatter_block, 0)

    every = pl.ds(0, segments - 1)
    pltpu.make_async_copy(total_in.at[every], total_in.at[every], trecv_sem).wait()
    inverse_rows(total_in)

    def arrived(at, piece):
        pltpu.make_async_copy(at, at, recv_sem.at[piece]).wait()

    def attend_unit(unit, carry):
        @pl.when(unit == 0)
        def _():
            arrived(inbox.at[0, every, :, pl.ds(0, STRIP)], 0)
            arrived(inbox.at[0, every, :, pl.ds(STRIP, STRIP)], 1)

        @pl.when(lax.rem(unit, 2) == 1)
        def _():
            arrived(inbox.at[pl.ds(unit, 2), every], (unit + 3) // 2)

        def store_arrived(at, groups, local, value):
            att_ref[at, local] = value.astype(bf16)

        first = unit * UNIT
        attend(
            lambda groups, local: inbox[unit, groups, :, local], store_arrived,
            inv_ref, cos_ref, sin_ref, bias_ref, scale_ref, first,
        )
        placed_ref[:, pl.ds(pl.multiple_of(first, UNIT), UNIT)] = jnp.dot(
            scatter_ref[...], att_ref[...], preferred_element_type=f32
        ).astype(bf16)
        return carry

    lax.fori_loop(0, units - 1, attend_unit, 0)
    arrived(last_ref.at[every], pairs)

    for u in range(strips):
        exchange(u).wait_send()
    sent = outbox.at[:, every]
    pltpu.make_async_copy(sent, sent, send_sem).wait()
    pltpu.make_async_copy(total.at[every], total.at[every], tsend_sem).wait()


def finish(placed_ref, last_ref, scatter_ref, out_ref, tail_ref, copy_sem):
    rows, width = placed_ref.shape
    done = width - UNIT
    early = pltpu.make_async_copy(
        placed_ref.at[:, pl.ds(0, done)], out_ref.at[:, pl.ds(0, done)], copy_sem.at[0]
    )
    early.start()
    arrived = last_ref[...].astype(jnp.float32).reshape(rows, UNIT).astype(jnp.bfloat16)
    tail_ref[...] = jnp.dot(
        scatter_ref[...], arrived, preferred_element_type=jnp.float32
    ).astype(jnp.bfloat16)
    late = pltpu.make_async_copy(tail_ref, out_ref.at[:, pl.ds(done, UNIT)], copy_sem.at[1])
    late.start()
    early.wait()
    late.wait()


def local(partials, kept_positions, destination, slot_index, query_scale, key_scale):
    f32, bf16 = jnp.float32, jnp.bfloat16
    rows, full = partials.shape[2:]
    width = full // 2
    units = width // UNIT
    segments = destination.shape[0]
    side = round(segments ** (1 / 3))
    freq = np.exp(np.arange(HD // 2, dtype=np.float32) * np.float32(-2.0 * math.log(THETA) / HD))
    freq = jnp.asarray(np.concatenate([freq, freq])[None, :].astype(np.float32))
    vmem = pl.BlockSpec(memory_space=pltpu.VMEM)
    hbm = pl.BlockSpec(memory_space=pltpu.HBM)
    sem = pltpu.SemaphoreType.DMA
    strips = 2 * units
    ints = pltpu.VMEM(destination.shape, jnp.int32)
    table = pltpu.VMEM((rows, HD), f32)
    square = pltpu.VMEM((rows, rows), bf16)
    sums = pltpu.VMEM((segments, 1, HD), f32)
    parts = pl.pallas_call(
        functools.partial(kernel, side, rows, width),
        out_shape=[
            pltpu.VMEM((rows, width), bf16),
            pltpu.VMEM((segments, CAP, UNIT), bf16),
            square,
        ],
        in_specs=[hbm] * 7,
        out_specs=[vmem] * 3,
        scratch_shapes=[
            ints, ints, ints,
            pltpu.VMEM((1, width), f32),
            pltpu.VMEM((1, width), f32),
            pltpu.VMEM((1, HD), f32),
            pltpu.VMEM((strips, rows, STRIP), bf16),
            pltpu.VMEM((strips, rows, STRIP), bf16),
            pltpu.VMEM((units, segments, CAP, UNIT), bf16),
            pltpu.VMEM((units - 1, segments, CAP, UNIT), bf16),
            square, square,
            pltpu.VMEM((segments, rows), f32),
            table, table, table, pltpu.VMEM((rows, BLOCK), f32),
            pltpu.VMEM((8, width), f32),
            table, table, table,
            sums, sums, sums, sums,
            pltpu.VMEM((rows, UNIT), bf16),
            sem((strips,)), sem((strips,)), sem((strips,)),
            sem, sem((units // 2 + 2,)),
            sem, sem, sem, sem,
            sem((6,)),
        ],
        compiler_params=pltpu.CompilerParams(
            collective_id=0, has_side_effects=True, vmem_limit_bytes=36 * 2**20
        ),
        name="handoff",
    )(*(
        pltpu.with_memory_space_constraint(array, pltpu.HBM)
        for array in (
            partials.reshape(rows, full), kept_positions, destination, slot_index,
            query_scale[None, :], key_scale[None, :], freq,
        )
    ))
    return pl.pallas_call(
        finish,
        out_shape=jax.ShapeDtypeStruct((rows, width), bf16),
        in_specs=[vmem] * 3,
        out_specs=pl.BlockSpec(memory_space=pl.ANY),
        scratch_shapes=[
            pltpu.VMEM((rows, UNIT), bf16),
            sem((2,)),
        ],
        compiler_params=pltpu.CompilerParams(vmem_limit_bytes=16 * 2**20),
        name="finish",
    )(*(pltpu.with_memory_space_constraint(part, pltpu.VMEM) for part in parts))


def solution(mesh):
    in_specs = (P("section", "tp", None, None), P(), P(), P(), P("tp"), P("tp"))
    return jax.shard_map(
        local, mesh=mesh, in_specs=in_specs,
        out_specs=P("section", "tp"), check_vma=False,
    )
```

time: 64.7 us -> 62.8 us (0.971)
  local copies, waits for them, and re-layouts: 2.02 us -> 0 us
    unnamed x1 -> x0, local copies, waits for them, and re-layouts: 2.02 us -> none
    pallas_call x1 -> x2, Pallas kernels: 62.6 us -> 62.7 us  [the longest x1 60.7 us: local(): pl.pallas_call(functools.partial(kernel, side, rows, width), out_shape=[p...]
where the time goes in v3:
time: 62.8 us; the launch traced here: 62.7 us
  Pallas kernels  62.7 us (100%)
    pallas_call x1, Pallas kernels, local(): pl.pallas_call(functools.partial(kernel, side, rows, width), out_shape=[p...  60.7 us
    pallas_call x1, Pallas kernels, local(): pl.pallas_call(finish, out_shape=jax.ShapeDtypeStruct((rows, width), bf16...  2.04 us

profile of v3, /device:TPU:1, one launch (start us, length us, event | category | flops | bytes accessed | tf_op | source)
XLA Modules:
  0.0 62.7 jit_solution(11734324358207977890)
XLA Ops:
  0.0 60.7 %handoff.1 = (bf16[512,4096]{1,0:T(8,128)(2,1)S(1)}, bf16[64,8,512]{2,1,0:T(8,128)(2,1)S(1)}, bf16[512,512]{1,0:T(8,128)(2,1)S(1)}) custom-call(bf16[512,8192]{1,0:T(8,128)(2,1)} %bitcast.3, s32[64,512]{1,0:T(8,128)} %pos_in.1, s32[64,512]{1,0:T(8,128)} %dest_in.1, s32[64,512]{1,0:T(8,128)} %slot_in.1, f32[1,4096]{1,0:T(1,128)} %bitcast.4, ...), custom_call_target="tpu_custom_call" | custom-call | tf_op jit(solution)/shard_map/handoff/pallas_call | solution.py:402
  60.7 2.0 %finish.1 = bf16[512,4096]{1,0:T(8,128)(2,1)} custom-call(bf16[512,4096]{1,0:T(8,128)(2,1)S(1)} %get-tuple-element.8.placed_ref, bf16[64,8,512]{2,1,0:T(8,128)(2,1)S(1)} %get-tuple-element.9.last_ref, bf16[512,512]{1,0:T(8,128)(2,1)S(1)} %get-tuple-element.10.scatter_ref), custom_call_target="tpu_custom_call" | custom-call | tf_op jit(solution)/shard_map/finish/pallas_call | solution.py:443

commit v4 on v3

--- a/solution.py
+++ b/solution.py
@@ -92,10 +92,12 @@
     part_ref, pos_in, dest_in, slot_in, qscale_in, kscale_in, freq_in,
     placed_ref, last_ref, scatter_ref,
     dest_ref, pos_ref, slot_ref, qscale_ref, kscale_ref, freq_ref,
+    near, raw_out, raw_in, raw_other,
     own, recv, outbox, inbox, before_ref, gather_ref, key_ref,
     inv_ref, cos_ref, sin_ref, bias_ref, scale_ref,
     posb, slotb, acc, half, half_in, total, total_in, att_ref,
     own_sem, xsend_sem, xrecv_sem, send_sem, recv_sem, hsend_sem, hrecv_sem, tsend_sem, trecv_sem, load_sem,
+    near_sem, raw_send_sem, raw_recv_sem, swap_send_sem, swap_recv_sem,
 ):
     f32, bf16 = jnp.float32, jnp.bfloat16
     segments = side ** 3
@@ -110,7 +112,7 @@
 
     def each_peer(act):
         for offset in order:
-            at = [lax.rem(h + o, side) for h, o in zip((z, y, x), offset)]
+            at = [lax.rem(h + side + o + tp * (side - 2 * o), side) for h, o in zip((z, y, x), offset)]
             act((at[0] * side + at[1]) * side + at[2])
 
     barrier = pltpu.get_barrier_semaphore()
@@ -136,9 +138,16 @@
             (qscale_in, qscale_ref), (kscale_in, kscale_ref), (freq_in, freq_ref),
         ))
     ]
-    for load in loads:
+    loads[0].start()
+    nears = [
+        pltpu.make_async_copy(
+            part_ref.at[:, pl.ds(pl.multiple_of(side_of * width, UNIT), HD)], near.at[:, pl.ds(i * HD, HD)], near_sem.at[i]
+        )
+        for i, side_of in enumerate((tp, other))
+    ]
+    for load in nears:
         load.start()
-    for u in range(strips):
+    for u in range(2):
         own_copy(u).start()
 
     before_ref[...] = (
@@ -155,21 +164,41 @@
     ).astype(f32).astype(bf16)
     acc[...] = jnp.zeros_like(acc)
 
+    for load in nears:
+        load.wait()
+    moved = jnp.dot(gather_ref[...], near[...], preferred_element_type=f32)
+    for i in range(2):
+        raw_out[i] = moved[:, i * HD:(i + 1) * HD].reshape(segments, CAP, HD).astype(bf16)
+    raw_in[:, pl.ds(me, 1)] = raw_out[:, pl.ds(me, 1)]
+
     pl.semaphore_wait(barrier, segments)
-    for u in range(2):
-        exchange(u).start()
+    exchange(0).start()
+
+    def send_raw(there):
+        pltpu.make_async_remote_copy(
+            src_ref=raw_out.at[:, there], dst_ref=raw_in.at[:, me], send_sem=raw_send_sem, recv_sem=raw_recv_sem,
+            device_id=(there, tp), device_id_type=MESH,
+        ).start()
+
+    each_peer(send_raw)
+    for u in range(2, strips):
+        own_copy(u).start()
+    for load in loads[1:]:
+        load.start()
 
     def send(source, target, piece):
+        sender = send_sem.at[0 if isinstance(piece, int) and piece < 2 else 1]
+
         def one(there):
             pltpu.make_async_remote_copy(
-                src_ref=source(there), dst_ref=target, send_sem=send_sem, recv_sem=recv_sem.at[piece],
+                src_ref=source(there), dst_ref=target, send_sem=sender, recv_sem=recv_sem.at[piece],
                 device_id=(there, tp), device_id_type=MESH,
             ).start()
 
         each_peer(one)
 
     def send_half(i):
-        columns = pl.ds(i * STRIP, STRIP)
+        columns = (pl.ds(HD, HD), pl.ds(STRIP, STRIP))[i]
         send(lambda there: outbox.at[0, there, :, columns], inbox.at[0, me, :, columns], i)
 
     def send_pair(p, carry):
@@ -181,9 +210,14 @@
         own_copy(u).wait()
         exchange(u).wait_recv()
 
-        @pl.when(u + 2 < strips)
+        @pl.when(u == 0)
         def _():
-            exchange(u + 2).start()
+            exchange(1).start()
+            exchange(2).start()
+
+        @pl.when(u + 3 < strips)
+        def _():
+            exchange(u + 3).start()
 
         unit = u // 2
         columns = pl.ds(pl.multiple_of(lax.rem(u, 2) * STRIP, STRIP), STRIP)
@@ -201,7 +235,14 @@
     lax.fori_loop(2, 6, reduce_strip, 0)
     send_pair(2, 0)
     lax.fori_loop(6, 10, reduce_strip, 0)
-    send_pair(3,0)
+    send_pair(3, 0)
+    every = pl.ds(0, segments - 1)
+    pltpu.make_async_copy(raw_in.at[:, every], raw_in.at[:, every], raw_recv_sem).wait()
+    swap = pltpu.make_async_remote_copy(
+        src_ref=raw_in.at[1], dst_ref=raw_other, send_sem=swap_send_sem, recv_sem=swap_recv_sem,
+        device_id=(me, other), device_id_type=MESH,
+    )
+    swap.start()
     lax.fori_loop(10, strips, reduce_strip, 0)
     mine_too = pl.ds(me, 1)
     inbox[:, mine_too] = outbox[pl.ds(0, units - 1), mine_too]
@@ -335,7 +376,9 @@
     def attend_unit(unit, carry):
         @pl.when(unit == 0)
         def _():
-            arrived(inbox.at[0, every, :, pl.ds(0, STRIP)], 0)
+            arrived(inbox.at[0, every, :, pl.ds(HD, HD)], 0)
+            swap.wait_recv()
+            inbox[0, :, :, 0:HD] = (raw_in[0].astype(f32) + raw_other[...].astype(f32)).astype(bf16)
             arrived(inbox.at[0, every, :, pl.ds(STRIP, STRIP)], 1)
 
         @pl.when(lax.rem(unit, 2) == 1)
@@ -360,8 +403,10 @@
 
     for u in range(strips):
         exchange(u).wait_send()
-    sent = outbox.at[:, every]
-    pltpu.make_async_copy(sent, sent, send_sem).wait()
+    swap.wait_send()
+    pltpu.make_async_copy(raw_out.at[:, every], raw_out.at[:, every], raw_send_sem).wait()
+    for i, sent in enumerate((outbox.at[0, every, :, pl.ds(HD, UNIT - HD)], outbox.at[pl.ds(1, units - 1), every])):
+        pltpu.make_async_copy(sent, sent, send_sem.at[i]).wait()
     pltpu.make_async_copy(total.at[every], total.at[every], tsend_sem).wait()
 
 
@@ -413,6 +458,10 @@
             pltpu.VMEM((1, width), f32),
             pltpu.VMEM((1, width), f32),
             pltpu.VMEM((1, HD), f32),
+            pltpu.VMEM((rows, 2 * HD), bf16),
+            pltpu.VMEM((2, segments, CAP, HD), bf16),
+            pltpu.VMEM((2, segments, CAP, HD), bf16),
+            pltpu.VMEM((segments, CAP, HD), bf16),
             pltpu.VMEM((strips, rows, STRIP), bf16),
             pltpu.VMEM((strips, rows, STRIP), bf16),
             pltpu.VMEM((units, segments, CAP, UNIT), bf16),
@@ -425,9 +474,10 @@
             sums, sums, sums, sums,
             pltpu.VMEM((rows, UNIT), bf16),
             sem((strips,)), sem((strips,)), sem((strips,)),
-            sem, sem((units // 2 + 2,)),
+            sem((2,)), sem((units // 2 + 2,)),
             sem, sem, sem, sem,
             sem((6,)),
+            sem((2,)), sem, sem, sem, sem,
         ],
         compiler_params=pltpu.CompilerParams(
             collective_id=0, has_side_effects=True, vmem_limit_bytes=36 * 2**20

time: 62.8 us -> 62.1 us (0.989)
  Pallas kernels: 62.7 us -> 62 us
    pallas_call x1, Pallas kernels: 60.7 us -> 59.9 us  [local(): pl.pallas_call(functools.partial(kernel, side, rows, width), out_shape=[p...]
where the time goes in v4:
time: 62.1 us; the launch traced here: 62 us
  Pallas kernels  62 us (100%)
    pallas_call x1, Pallas kernels, local(): pl.pallas_call(functools.partial(kernel, side, rows, width), out_shape=[p...  59.9 us
    pallas_call x1, Pallas kernels, local(): pl.pallas_call(finish, out_shape=jax.ShapeDtypeStruct((rows, width), bf16...  2.04 us

profile of v4, /device:TPU:1, one launch (start us, length us, event | category | flops | bytes accessed | tf_op | source)
XLA Modules:
  0.0 62.0 jit_solution(12783214314359328783)
XLA Ops:
  0.0 59.9 %handoff.1 = (bf16[512,4096]{1,0:T(8,128)(2,1)S(1)}, bf16[64,8,512]{2,1,0:T(8,128)(2,1)S(1)}, bf16[512,512]{1,0:T(8,128)(2,1)S(1)}) custom-call(bf16[512,8192]{1,0:T(8,128)(2,1)} %bitcast.3, s32[64,512]{1,0:T(8,128)} %pos_in.1, s32[64,512]{1,0:T(8,128)} %dest_in.1, s32[64,512]{1,0:T(8,128)} %slot_in.1, f32[1,4096]{1,0:T(1,128)} %bitcast.4, ...), custom_call_target="tpu_custom_call" | custom-call | tf_op jit(solution)/shard_map/handoff/pallas_call | solution.py:447
  59.9 2.0 %finish.1 = bf16[512,4096]{1,0:T(8,128)(2,1)} custom-call(bf16[512,4096]{1,0:T(8,128)(2,1)S(1)} %get-tuple-element.8.placed_ref, bf16[64,8,512]{2,1,0:T(8,128)(2,1)S(1)} %get-tuple-element.9.last_ref, bf16[512,512]{1,0:T(8,128)(2,1)S(1)} %get-tuple-element.10.scatter_ref), custom_call_target="tpu_custom_call" | custom-call | tf_op jit(solution)/shard_map/finish/pallas_call | solution.py:493

commit v5 on v4

--- a/solution.py
+++ b/solution.py
@@ -197,9 +197,9 @@
 
         each_peer(one)
 
-    def send_half(i):
-        columns = (pl.ds(HD, HD), pl.ds(STRIP, STRIP))[i]
-        send(lambda there: outbox.at[0, there, :, columns], inbox.at[0, me, :, columns], i)
+    def send_rest():
+        columns = pl.ds(HD, UNIT - HD)
+        send(lambda there: outbox.at[0, there, :, columns], inbox.at[0, me, :, columns], 0)
 
     def send_pair(p, carry):
         two = pl.ds(2 * p - 3, 2)
@@ -228,10 +228,8 @@
         acc[...] += square[:, :HD] + square[:, HD:]
         return carry
 
-    lax.fori_loop(0, 1, reduce_strip, 0)
-    send_half(0)
-    lax.fori_loop(1, 2, reduce_strip, 0)
-    send_half(1)
+    lax.fori_loop(0, 2, reduce_strip, 0)
+    send_rest()
     lax.fori_loop(2, 6, reduce_strip, 0)
     send_pair(2, 0)
     lax.fori_loop(6, 10, reduce_strip, 0)
@@ -376,10 +374,9 @@
     def attend_unit(unit, carry):
         @pl.when(unit == 0)
         def _():
-            arrived(inbox.at[0, every, :, pl.ds(HD, HD)], 0)
+            arrived(inbox.at[0, every, :, pl.ds(HD, UNIT - HD)], 0)
             swap.wait_recv()
             inbox[0, :, :, 0:HD] = (raw_in[0].astype(f32) + raw_other[...].astype(f32)).astype(bf16)
-            arrived(inbox.at[0, every, :, pl.ds(STRIP, STRIP)], 1)
 
         @pl.when(lax.rem(unit, 2) == 1)
         def _():
@@ -399,15 +396,15 @@
         return carry
 
     lax.fori_loop(0, units - 1, attend_unit, 0)
-    arrived(last_ref.at[every], pairs)
-
     for u in range(strips):
         exchange(u).wait_send()
     swap.wait_send()
     pltpu.make_async_copy(raw_out.at[:, every], raw_out.at[:, every], raw_send_sem).wait()
+    pltpu.make_async_copy(total.at[every], total.at[every], tsend_sem).wait()
+    arrived(last_ref.at[every], pairs)
+
     for i, sent in enumerate((outbox.at[0, every, :, pl.ds(HD, UNIT - HD)], outbox.at[pl.ds(1, units - 1), every])):
         pltpu.make_async_copy(sent, sent, send_sem.at[i]).wait()
-    pltpu.make_async_copy(total.at[every], total.at[every], tsend_sem).wait()
 
 
 def finish(placed_ref, last_ref, scatter_ref, out_ref, tail_ref, copy_sem):

time: 62.1 us -> 62.2 us (level)
  no operation moved by 1% of the time
where the time goes in v5:
time: 62.2 us; the launch traced here: 62.1 us
  Pallas kernels  62.1 us (100%)
    pallas_call x1, Pallas kernels, local(): pl.pallas_call(functools.partial(kernel, side, rows, width), out_shape=[p...  60 us
    pallas_call x1, Pallas kernels, local(): pl.pallas_call(finish, out_shape=jax.ShapeDtypeStruct((rows, width), bf16...  2.04 us

profile of v5, /device:TPU:1, one launch (start us, length us, event | category | flops | bytes accessed | tf_op | source)
XLA Modules:
  0.0 62.1 jit_solution(6393564469215769027)
XLA Ops:
  0.0 60.0 %handoff.1 = (bf16[512,4096]{1,0:T(8,128)(2,1)S(1)}, bf16[64,8,512]{2,1,0:T(8,128)(2,1)S(1)}, bf16[512,512]{1,0:T(8,128)(2,1)S(1)}) custom-call(bf16[512,8192]{1,0:T(8,128)(2,1)} %bitcast.3, s32[64,512]{1,0:T(8,128)} %pos_in.1, s32[64,512]{1,0:T(8,128)} %dest_in.1, s32[64,512]{1,0:T(8,128)} %slot_in.1, f32[1,4096]{1,0:T(1,128)} %bitcast.4, ...), custom_call_target="tpu_custom_call" | custom-call | tf_op jit(solution)/shard_map/handoff/pallas_call | solution.py:444
  60.0 2.0 %finish.1 = bf16[512,4096]{1,0:T(8,128)(2,1)} custom-call(bf16[512,4096]{1,0:T(8,128)(2,1)S(1)} %get-tuple-element.8.placed_ref, bf16[64,8,512]{2,1,0:T(8,128)(2,1)S(1)} %get-tuple-element.9.last_ref, bf16[512,512]{1,0:T(8,128)(2,1)S(1)} %get-tuple-element.10.scatter_ref), custom_call_target="tpu_custom_call" | custom-call | tf_op jit(solution)/shard_map/finish/pallas_call | solution.py:490
